TPU v7x, 32 devices: a whole 2x2x4 slice. The times are simulated.
32 devices in a mesh: groups: 2 (over y), tm: 4 (over z), comp: 2 (over core), panel: 2 (over x).
Axes of the slice: x: 2, y: 2, z: 4, core: 2. Of those that a mesh axis runs over, the one named last changes fastest.
Arguments:
- orbit_angles: float32 [2, 8192], P(None, ('groups', 'tm')), parts along dimension 1, may hold values from -3.15 to 3.15, as said below
- gap_mask: int32 [8192], P(('groups', 'tm')), parts along dimension 0, may hold values 0 or 1
- column_index: int32 [2, 512], P(None, 'panel'), may hold values from -280 to 280, as said below
- lat_coeffs: bfloat16 [2, 640, 512], P('comp', None, 'panel'), may hold values from -6 to 6
- psd_table: int32 [2, 2049], P('comp'), may hold values from 1024 to 32752, as said below
Outputs:
- normals: float32 [1024, 512], P(('groups', 'tm'), 'panel'), parts along dimension 0
There are 2 independent parts, one for each index of `groups`. A program takes and returns all parts, laid end to end along the dimension named above; an argument that names none is the same for every part. Nothing has to cross between parts.
Inputs may be any that keep to these rules, and one draw needn't show every extreme that they name: orbit_angles holds colatitude in its first row and longitude in its second. `column_index`: the first row holds each unknown's degree, the second its order; a degree is at least 2 and at least the order's magnitude; a negative order stands for the sine term in longitude. `psd_table`: entry g of a component's row is its noise power at frequency g (and 4096 - g), times 8192.
All inputs are finite; a program needn't handle non-finite values. No bound on the sum of `gap_mask` on one device may be relied on, other than what follows from the above.
Results may differ from a plain program's by a relative error of at most 0.0016.
Values may be sent and summed in bfloat16 or wider, within the bound.
A program may use at most 64 MiB of HBM per device.

v0:
```python
import functools
import math

import jax
import jax.numpy as jnp
import numpy as np
from jax import lax
from jax.experimental import pallas as pl
from jax.experimental.pallas import tpu as pltpu
from jax.sharding import PartitionSpec as P

SPLIT = 64


def synthesize(angles, keep_rows, column_index, coeffs):
    terms_lat = coeffs.shape[0] // 2
    colatitude = angles[0]
    longit = angles[1]
    wavenumbers = jnp.arange(terms_lat, dtype=jnp.float32)
    phases = colatitude[:, None] * wavenumbers[None, :]
    basis_rows = jnp.concatenate([jnp.cos(phases), jnp.sin(phases)], axis=1).astype(jnp.bfloat16)
    degree = column_index[0]
    orders = column_index[1]
    levels = jnp.arange(2 * terms_lat, dtype=jnp.int32) % terms_lat
    allowed = levels[:, None] <= degree[None, :]
    masked = jnp.where(allowed, coeffs, jnp.zeros_like(coeffs))
    latitude = jnp.dot(basis_rows, masked, preferred_element_type=jnp.float32)
    lon_phase = longit[:, None] * jnp.abs(orders).astype(jnp.float32)[None, :]
    lon_wave = jnp.where(orders[None, :] >= 0, jnp.cos(lon_phase), jnp.sin(lon_phase))
    norm_scale = 1.0 / jnp.sqrt(degree.astype(jnp.float32) + 1.0)
    return latitude * lon_wave * (keep_rows[:, None] * norm_scale[None, :])


def phase_tables(row_index, col_index, length):
    product = row_index[:, None] * col_index[None, :] % length
    angle_grid = product.astype(jnp.float32) * (2.0 * math.pi / length)
    return (jnp.cos(angle_grid), jnp.sin(angle_grid))


def dft_tables(length):
    indices = jnp.arange(length, dtype=jnp.int32)
    return phase_tables(indices, indices, length)


def rotate(real_part, imag_part, outer_index, inner_index, length):
    index_grid = outer_index[:, None] * inner_index[None, :] % length
    angle_grid = index_grid.astype(jnp.float32) * (2.0 * math.pi / length)
    cosine = jnp.cos(angle_grid)[:, :, None]
    sine_grid = jnp.sin(angle_grid)[:, :, None]
    return (real_part * cosine + imag_part * sine_grid, imag_part * cosine - real_part * sine_grid)


def precise_dot(left_side, right_side):
    return jnp.dot(
        left_side, right_side, precision=lax.Precision.HIGHEST, preferred_element_type=jnp.float32
    )


def transform(cos_table, sin_table, real_part, imag_part):
    new_real = precise_dot(cos_table, real_part) + precise_dot(sin_table, imag_part)
    new_imag = precise_dot(cos_table, imag_part) - precise_dot(sin_table, real_part)
    return (new_real, new_imag)


def four_step(real_in, imag_in, samples):
    length = real_in.shape[0]
    columns = real_in.shape[1]
    outer_count = SPLIT
    inner_count = length // SPLIT
    real_part = real_in.reshape(outer_count, inner_count * columns)
    imag_part = imag_in.reshape(outer_count, inner_count * columns)
    cos_outer, sin_outer = dft_tables(outer_count)
    real_part, imag_part = transform(cos_outer, sin_outer, real_part, imag_part)
    real_part = real_part.reshape(outer_count, inner_count, columns)
    imag_part = imag_part.reshape(outer_count, inner_count, columns)
    real_part, imag_part = rotate(
        real_part,
        imag_part,
        jnp.arange(outer_count, dtype=jnp.int32),
        jnp.arange(inner_count, dtype=jnp.int32),
        length,
    )
    real_part = jnp.transpose(real_part, (1, 0, 2)).reshape(inner_count, outer_count * columns)
    imag_part = jnp.transpose(imag_part, (1, 0, 2)).reshape(inner_count, outer_count * columns)
    cos_inner, sin_inner = dft_tables(inner_count)
    real_part, imag_part = transform(cos_inner, sin_inner, real_part, imag_part)
    return (
        real_part.reshape(length, columns) / samples,
        imag_part.reshape(length, columns) / samples,
    )


def local_transform(received, samples):
    real_part, imag_part = four_step(received[0, 0], received[1, 0], samples)
    return (real_part.astype(jnp.bfloat16), imag_part.astype(jnp.bfloat16))


def noise_weighted(spectra, psd_row, frequency, samples):
    folded = jnp.minimum(frequency, samples - frequency)
    inverse_psd = 8192.0 / jnp.take(psd_row, folded).astype(jnp.float32)
    return (spectra.astype(jnp.float32) * inverse_psd[None, :, None]).astype(jnp.bfloat16)


def settle(partial_value, sum_dim):
    summed = lax.psum_scatter(partial_value, "tm", scatter_dimension=sum_dim, tiled=True)
    return lax.psum(summed, "comp")


def body(orbit_angles, gap_mask, column_index, lat_coeffs, psd_table):
    devices_tm = lax.axis_size("tm")
    epochs = orbit_angles.shape[1]
    block_len = epochs // devices_tm
    samples = epochs * devices_tm
    columns = lat_coeffs.shape[2]
    coeffs = lat_coeffs[0]
    keep_rows = gap_mask.astype(jnp.float32)
    packed = jnp.concatenate([orbit_angles, keep_rows[None]], axis=0)[:, None, :]
    received = lax.all_to_all(packed, "tm", split_axis=2, concat_axis=1, tiled=True)
    flat_orbit = received.reshape(3, devices_tm * block_len)
    spread = synthesize(flat_orbit[0:2], flat_orbit[2], column_index, coeffs).reshape(
        devices_tm, block_len, columns
    )
    position = lax.axis_index("tm")
    local_epoch = position * block_len + jnp.arange(block_len, dtype=jnp.int32)
    cos_outer, sin_outer = dft_tables(devices_tm)
    flat_design = spread.reshape(devices_tm, block_len * columns)
    real_part = precise_dot(cos_outer, flat_design).reshape(devices_tm, block_len, columns)
    imag_part = -precise_dot(sin_outer, flat_design).reshape(devices_tm, block_len, columns)
    real_part, imag_part = rotate(
        real_part, imag_part, jnp.arange(devices_tm, dtype=jnp.int32), local_epoch, samples
    )
    twisted = jnp.stack([real_part, imag_part])
    spec_real, spec_imag = local_transform(
        lax.all_to_all(twisted, "tm", split_axis=1, concat_axis=2, tiled=True), samples
    )
    spectra = jnp.stack([spec_real, spec_imag])
    psd_row = psd_table[0]
    contract = (((0, 1), (0, 1)), ((), ()))
    frequency = position + devices_tm * jnp.arange(epochs, dtype=jnp.int32)
    weighted = noise_weighted(spectra, psd_row, frequency, samples)
    partial_value = lax.dot_general(
        lax.all_gather(spectra, "panel", axis=2, tiled=True),
        weighted,
        contract,
        preferred_element_type=jnp.float32,
    )
    return settle(partial_value, 0)


RADIX = 16
SINE_LON = (6.283164044168851, -41.33714234995496, 81.34076808172247, -70.99342472149007)
SINE_FINE = (
    6.283185160088548,
    -41.3416550311802,
    81.60100405747373,
    -76.54978191007581,
    39.53670300634923,
)
CLASSES = (2, 4, 6, 1, 5, 9, 13)
EVEN = 3
MESH = pl.DeviceIdType.MESH


def cos_turns(turns, terms=SINE_FINE):
    offset = turns - jnp.round(turns)
    near = 0.25 - jnp.abs(offset)
    square = near * near
    total = terms[-1]
    for term in terms[-2::-1]:
        total = total * square + term
    return total * near


def iota(shape, dim):
    return lax.broadcasted_iota(jnp.int32, shape, dim)


def split(value):
    high = value.astype(jnp.bfloat16)
    return high, (value - high.astype(jnp.float32)).astype(jnp.bfloat16)


def tables(length):
    samples = RADIX * length
    half = length // 2

    def waves(product):
        angle = (product % samples) * (2.0 * np.pi / samples)
        return np.cos(angle), np.sin(angle)

    count = np.arange(length)
    cosine, sine = waves(RADIX * np.outer(count, count))
    zero = np.concatenate([cosine[:, :half], -sine[:, :half]], axis=1)
    zero[:, half] = 1 - 2 * (count % 2)
    eight = np.concatenate(waves(np.outer(count, RADIX // 2 + RADIX * count[:half])), axis=1)
    eight[:, half:] *= -1
    turn = [wave for cls in CLASSES for wave in waves(cls * count)]
    square = np.stack([cosine, sine, zero, eight]) / samples
    return square.astype(np.float32), np.stack(turn).astype(np.float32)


def put_matrix(ref, at, value, lanes):
    high, low = split(value)
    third = ref.shape[0] // 3
    for block, part in ((0, high), (1, high), (2, low)):
        start = block * third + at
        ref[start : start + value.shape[0], lanes] = part


def put_rows(ref, slot, rows, at, value):
    high, low = split(value)
    past = ref.shape[2] // 2 + at
    ref[slot, rows, at : at + value.shape[1]] = high
    ref[slot, rows, past : past + value.shape[1]] = low


def frequency_weights(psd_ref, wts_ref, samples):
    length = samples // RADIX
    half = length // 2
    power = jnp.concatenate([psd_ref[:, half * i : half * (i + 1)] for i in range(RADIX)], axis=0)
    spread = (iota((RADIX, half), 0) == iota((RADIX, half), 1) >> 3).astype(jnp.bfloat16)
    keep = (iota((half, half), 0) >> 4) == (iota((half, half), 1) & (half // RADIX - 1))
    pick_up = ((iota((RADIX, half), 1) & (RADIX - 1)) == iota((RADIX, half), 0)).astype(jnp.bfloat16)
    pick_down = ((iota((RADIX, half), 1) + iota((RADIX, half), 0)) & (RADIX - 1) == 0).astype(
        jnp.bfloat16
    )
    flip = (iota((half, half), 0) + iota((half, half), 1) == half - 1).astype(jnp.bfloat16)
    up = jnp.zeros((RADIX, half), jnp.float32)
    down = jnp.zeros((RADIX, half), jnp.float32)
    for digits, unit in ((power >> 8, 256.0), (power & 255, 1.0)):
        digits = digits.astype(jnp.float32).astype(jnp.bfloat16)
        moved = lax.dot_general(
            digits, spread, (((0,), (0,)), ((), ())), preferred_element_type=jnp.float32
        )
        moved = jnp.where(keep, moved, 0.0).astype(jnp.bfloat16)
        up = up + unit * jnp.dot(pick_up, moved, preferred_element_type=jnp.float32)
        back = jnp.dot(pick_down, moved, preferred_element_type=jnp.float32).astype(jnp.bfloat16)
        down = down + unit * jnp.dot(back, flip, preferred_element_type=jnp.float32)
    up = 2.0 * (8192.0 / up)
    down = 2.0 * (8192.0 / down)
    last = 8192.0 / psd_ref[:, samples // 2 : samples // 2 + 1].astype(jnp.float32)
    first = iota((1, half), 1) == 0
    wts_ref[0:1, 0:half] = jnp.where(first, 0.5 * up[0:1], up[0:1])
    wts_ref[0:1, half:length] = jnp.where(first, last, up[0:1])
    wts_ref[1:2, 0:half] = up[RADIX // 2 : RADIX // 2 + 1]
    wts_ref[1:2, half:length] = up[RADIX // 2 : RADIX // 2 + 1]
    for slot, cls in enumerate(CLASSES):
        for at in (0, length):
            wts_ref[slot + 2 : slot + 3, at : at + half] = up[cls : cls + 1]
            wts_ref[slot + 2 : slot + 3, at + half : at + length] = down[cls : cls + 1]


def even_classes(d):
    r = math.sqrt(0.5)
    even, alt = [], []
    for q in range(4):
        first, second = d(q) + d(q + 8), d(q + 4) + d(q + 12)
        even.append(first + second)
        alt.append(first - second)
    e02, e13 = even[0] + even[2], even[1] + even[3]
    four = (even[0] - even[2], even[3] - even[1])
    p, q = r * (alt[1] - alt[3]), r * (alt[1] + alt[3])
    two = (alt[0] + p, -(alt[2] + q))
    six = (alt[0] - p, alt[2] - q)
    return (e02 + e13, e02 - e13), (two, four, six)


def odd_classes(d):
    br, bi = [], []
    for q in range(4):
        real, imag = d(q) - d(q + 8), d(q + 12) - d(q + 4)
        c, s = math.cos(math.pi * q / 8), math.sin(math.pi * q / 8)
        if q == 2:
            real, imag = c * (real + imag), c * (imag - real)
        elif q:
            real, imag = c * real + s * imag, c * imag - s * real
        br.append(real)
        bi.append(imag)
    sr, si = br[0] + br[2], bi[0] + bi[2]
    tr, ti = br[1] + br[3], bi[1] + bi[3]
    ur, ui = br[0] - br[2], bi[0] - bi[2]
    vr, vi = br[1] - br[3], bi[1] - bi[3]
    return (sr + tr, si + ti), (ur + vi, ui - vr), (sr - tr, si - ti), (ur - vi, ui + vr)


def kernel(
    devices_tm,
    angles_hbm,
    mask_hbm,
    columns_hbm,
    coeffs_hbm,
    psd_hbm,
    square_hbm,
    twiddle_hbm,
    own_ref,
    other_ref,
    angles_ref,
    mask_ref,
    columns_ref,
    coeffs_ref,
    psd_ref,
    orbit,
    far_coeffs,
    far_columns,
    coeffs_t,
    column_t,
    basis_a,
    basis_b,
    design,
    real,
    pair_even,
    pair_odd,
    mat_real,
    mat,
    square,
    twiddle,
    wts,
    total,
    send_sem,
    recv_sem,
    side_send,
    side_recv,
    load_sem,
):
    block = angles_ref.shape[1]
    samples = block * devices_tm
    length = samples // RADIX
    half = length // 2
    terms = coeffs_ref.shape[1]
    terms_lat = terms // 2
    columns = coeffs_ref.shape[2]
    rows = own_ref.shape[0]
    everyone = rows + columns
    me = lax.axis_index("tm")
    panel = lax.axis_index("panel")
    comp = lax.axis_index("comp")

    loads = [
        pltpu.make_async_copy(source, held, load_sem.at[i])
        for i, (source, held) in enumerate(
            (
                (angles_hbm, angles_ref),
                (mask_hbm, mask_ref),
                (columns_hbm, columns_ref),
                (coeffs_hbm, coeffs_ref),
                (psd_hbm, psd_ref),
                (twiddle_hbm, twiddle),
                (square_hbm, square),
            )
        )
    ]
    for load in loads:
        load.start()
    barrier = pltpu.get_barrier_semaphore()
    peers = [lax.rem(me + k, devices_tm) for k in range(1, devices_tm)]
    for peer in peers:
        pl.semaphore_signal(barrier, inc=1, device_id={"tm": peer}, device_id_type=MESH)
    pl.semaphore_signal(barrier, inc=1, device_id={"panel": 1 - panel}, device_id_type=MESH)
    pl.semaphore_signal(barrier, inc=1, device_id={"comp": 1 - comp}, device_id_type=MESH)

    loads[0].wait()
    loads[1].wait()
    orbit[me, 0:2, :] = angles_ref[...] * (0.5 / math.pi)
    orbit[me, 2:3, :] = mask_ref[...].astype(jnp.float32)
    pl.semaphore_wait(barrier, devices_tm + 1)

    def send_orbit(k, slot, peer):
        return pltpu.make_async_remote_copy(
            src_ref=orbit.at[slot],
            dst_ref=orbit.at[slot],
            send_sem=send_sem.at[k],
            recv_sem=recv_sem.at[slot],
            device_id={"tm": peer},
            device_id_type=MESH,
        )

    for k, peer in enumerate(peers):
        send_orbit(k, me, peer).start()
    first_row = me * rows
    lanes = pl.ds(pl.multiple_of(lax.rem(first_row, columns), rows), rows)
    send_coeffs = pltpu.make_async_remote_copy(
        src_ref=coeffs_hbm.at[0, :, lanes],
        dst_ref=far_coeffs,
        send_sem=side_send.at[0],
        recv_sem=side_recv.at[0],
        device_id={"panel": 1 - panel},
        device_id_type=MESH,
    )
    send_columns = pltpu.make_async_remote_copy(
        src_ref=columns_hbm.at[:, lanes],
        dst_ref=far_columns,
        send_sem=side_send.at[1],
        recv_sem=side_recv.at[1],
        device_id={"panel": 1 - panel},
        device_id_type=MESH,
    )
    send_coeffs.start()
    send_columns.start()

    loads[6].wait()
    left, right = slice(0, length), slice(length, 2 * length)
    put_matrix(mat, 0, square[0], left)
    put_matrix(mat, 0, -square[1], right)
    put_matrix(mat, length, square[1], left)
    put_matrix(mat, length, square[0], right)
    put_matrix(mat_real.at[0], 0, square[2], left)
    put_matrix(mat_real.at[1], 0, square[3], left)
    loads[4].wait()
    frequency_weights(psd_ref, wts, samples)

    def place(at, coeffs, index_rows):
        width = coeffs.shape[1]
        level = iota((terms, width), 0)
        level = jnp.where(level < terms_lat, level, level - terms_lat)
        masked = jnp.where(level <= index_rows[0:1, :], coeffs, 0.0)
        coeffs_t[at : at + width, :] = jnp.transpose(masked).astype(jnp.bfloat16)
        orders = index_rows[1:2, :]
        shift = jnp.where(orders >= 0, 0.0, 0.25)
        norm = 1.0 / jnp.sqrt(index_rows[0:1, :].astype(jnp.float32) + 1.0)
        packed = jnp.concatenate(
            [jnp.abs(orders).astype(jnp.float32), shift]
            + [norm * term for term in SINE_LON]
            + [jnp.zeros((2, width), jnp.float32)],
            axis=0,
        )
        turned = jnp.transpose(packed)
        for i in range(2 + len(SINE_LON)):
            column_t[i, at : at + width, :] = jnp.broadcast_to(turned[:, i : i + 1], (width, 128))

    loads[2].wait()
    loads[3].wait()
    place(0, coeffs_ref[0].astype(jnp.float32), columns_ref[...])
    send_coeffs.wait()
    send_columns.wait()
    mine = first_row // columns == panel
    near = coeffs_ref[0, :, lanes].astype(jnp.float32)
    place(
        columns,
        jnp.where(mine, near, far_coeffs[...].astype(jnp.float32)),
        jnp.where(mine, columns_ref[:, lanes], far_columns[...]),
    )
    for k, peer in enumerate(peers):
        send_orbit(k, me, peer).wait_send()
    for k, peer in enumerate(peers):
        send_orbit(k, peer, peer).wait_recv()

    per_device = block // length

    def epoch_rows(chunk):
        where = pl.ds(pl.multiple_of(lax.rem(chunk, per_device) * length, length), length)
        return orbit[chunk // per_device, :, where]

    def fill_basis(chunk, basis):
        part = epoch_rows(chunk)
        theta, keep = part[0:1], part[2:3]
        turns = iota((16, length), 0).astype(jnp.float32) * theta
        cosine, sine = cos_turns(turns) * keep, cos_turns(turns - 0.25) * keep
        step_c, step_s = cos_turns(16.0 * theta), cos_turns(16.0 * theta - 0.25)
        for at in range(0, terms_lat, 16):
            basis[at : at + 16, :] = cosine.astype(jnp.bfloat16)
            basis[terms_lat + at : terms_lat + at + 16, :] = sine.astype(jnp.bfloat16)
            cosine, sine = cosine * step_c - sine * step_s, sine * step_c + cosine * step_s

    def fill_design(chunk, basis):
        longit = epoch_rows(chunk)[1:2]
        latitude = jnp.dot(coeffs_t[...], basis[...], preferred_element_type=jnp.float32)
        terms_lon = [column_t[2 + i] for i in range(len(SINE_LON))]
        for lane in range(0, length, 128):
            lanes = slice(lane, lane + 128)
            wave = cos_turns(column_t[0] * longit[:, lanes] - column_t[1], terms_lon)
            design[chunk, :, lanes] = latitude[:, lanes] * wave

    fill_basis(0, basis_a)

    def two_chunks(i, carry):
        fill_basis(2 * i + 1, basis_b)
        fill_design(2 * i, basis_a)
        fill_basis(lax.rem(2 * i + 2, RADIX), basis_a)
        fill_design(2 * i + 1, basis_b)
        return carry

    lax.fori_loop(0, RADIX // 2, two_chunks, 0)

    def turn(slot, pair, at, lane, value):
        re, im = value
        c = twiddle[2 * slot : 2 * slot + 1, lane : lane + 128]
        s = twiddle[2 * slot + 1 : 2 * slot + 2, lane : lane + 128]
        place_at = slot if slot < EVEN else slot - EVEN
        put_rows(pair, place_at, at, lane, re * c + im * s)
        put_rows(pair, place_at, at, length + lane, im * c - re * s)

    def fold_even(i, carry):
        at = pl.ds(pl.multiple_of(i * 16, 16), 16)
        for lane in range(0, length, 128):
            plain, pairs = even_classes(lambda q: design[q, at, lane : lane + 128])
            for slot, value in enumerate(plain):
                put_rows(real, slot, at, lane, value)
            for slot, value in enumerate(pairs):
                turn(slot, pair_even, at, lane, value)
        return carry

    def fold_odd(i):
        at = pl.ds(pl.multiple_of(i * 16, 16), 16)
        for lane in range(0, length, 128):
            for slot, value in enumerate(odd_classes(lambda q: design[q, at, lane : lane + 128])):
                turn(EVEN + slot, pair_odd, at, lane, value)

    loads[5].wait()
    lax.fori_loop(0, everyone // 16, fold_even, 0)

    def gram(parts, matrix, weight):
        high = parts[:, : parts.shape[1] // 2]
        spectra = jnp.dot(
            jnp.concatenate([parts, high], axis=1), matrix, preferred_element_type=jnp.float32
        ).astype(jnp.bfloat16)
        weighted = (spectra[:columns].astype(jnp.float32) * weight).astype(jnp.bfloat16)
        return lax.dot_general(
            spectra[columns:], weighted, (((1,), (1,)), ((), ())), preferred_element_type=jnp.float32
        )

    total[...] = jnp.zeros_like(total)
    units = everyone // 16 // EVEN

    def even_step(slot, carry):
        total[...] += gram(pair_even[slot], mat[...], wts[pl.ds(slot + 2, 1), :])
        for unit in range(units):
            fold_odd(slot * units + unit)
        return carry

    def odd_step(slot, carry):
        total[...] += gram(pair_odd[slot], mat[...], wts[pl.ds(slot + 2 + EVEN, 1), :])
        return carry

    lax.fori_loop(0, EVEN, even_step, 0)
    lax.fori_loop(0, len(CLASSES) - EVEN, odd_step, 0)
    for slot in range(2):
        total[...] += gram(real[slot], mat_real[slot], wts[slot : slot + 1, 0:length])
    swap = pltpu.make_async_remote_copy(
        src_ref=total,
        dst_ref=other_ref,
        send_sem=side_send.at[2],
        recv_sem=side_recv.at[2],
        device_id={"comp": 1 - comp},
        device_id_type=MESH,
    )
    swap.start()
    own_ref[...] = total[...]
    swap.wait()


def fused(orbit_angles, gap_mask, column_index, lat_coeffs, psd_table):
    devices_tm = lax.axis_size("tm")
    block = orbit_angles.shape[1]
    samples = devices_tm * block
    length = samples // RADIX
    terms, columns = lat_coeffs.shape[1:]
    rows = columns * lax.axis_size("panel") // devices_tm
    everyone = rows + columns
    f32, bf16 = jnp.float32, jnp.bfloat16
    vmem = pl.BlockSpec(memory_space=pltpu.VMEM)
    count = len(CLASSES)
    own, other = pl.pallas_call(
        functools.partial(kernel, devices_tm),
        out_shape=[jax.ShapeDtypeStruct((rows, columns), f32)] * 2,
        in_specs=[pl.BlockSpec(memory_space=pltpu.HBM)] * 7,
        out_specs=[vmem] * 2,
        scratch_shapes=[
            pltpu.VMEM(orbit_angles.shape, f32),
            pltpu.VMEM((1, block), jnp.int32),
            pltpu.VMEM(column_index.shape, jnp.int32),
            pltpu.VMEM(lat_coeffs.shape, bf16),
            pltpu.VMEM(psd_table.shape, jnp.int32),
            pltpu.VMEM((devices_tm, 8, block), f32),
            pltpu.VMEM((terms, rows), bf16),
            pltpu.VMEM((2, rows), jnp.int32),
            pltpu.VMEM((everyone, terms), bf16),
            pltpu.VMEM((2 + len(SINE_LON), everyone, 128), f32),
            pltpu.VMEM((terms, length), bf16),
            pltpu.VMEM((terms, length), bf16),
            pltpu.VMEM((RADIX, everyone, length), f32),
            pltpu.VMEM((2, everyone, 2 * length), bf16),
            pltpu.VMEM((EVEN, everyone, 4 * length), bf16),
            pltpu.VMEM((count - EVEN, everyone, 4 * length), bf16),
            pltpu.VMEM((2, 3 * length, length), bf16),
            pltpu.VMEM((6 * length, 2 * length), bf16),
            pltpu.VMEM((4, length, length), f32),
            pltpu.VMEM((2 * count, length), f32),
            pltpu.VMEM((16, 2 * length), f32),
            pltpu.VMEM((rows, columns), f32),
            pltpu.SemaphoreType.DMA((devices_tm,)),
            pltpu.SemaphoreType.DMA((devices_tm,)),
            pltpu.SemaphoreType.DMA((3,)),
            pltpu.SemaphoreType.DMA((3,)),
            pltpu.SemaphoreType.DMA((7,)),
        ],
        compiler_params=pltpu.CompilerParams(
            collective_id=0, has_side_effects=True, vmem_limit_bytes=63 * 1024 * 1024
        ),
    )(orbit_angles, gap_mask.reshape(1, block), column_index, lat_coeffs, psd_table, *tables(length))
    return own + other


def choose(orbit_angles, gap_mask, column_index, lat_coeffs, psd_table):
    devices_tm, panels = lax.axis_size("tm"), lax.axis_size("panel")
    samples = devices_tm * orbit_angles.shape[1]
    columns = lat_coeffs.shape[2]
    rows = columns * panels // devices_tm
    fits = (
        samples == 4096
        and orbit_angles.shape[1] % 256 == 0
        and panels == 2
        and lax.axis_size("comp") == 2
        and rows % 128 == 0
        and columns % rows == 0
        and lat_coeffs.shape[1] % 32 == 0
        and (rows + columns) * lat_coeffs.shape[1] <= 512 * 1024
    )
    step = fused if fits else body
    return step(orbit_angles, gap_mask, column_index, lat_coeffs, psd_table)


def solution(mesh):
    return jax.shard_map(
        choose,
        mesh=mesh,
        in_specs=(
            P(None, ("groups", "tm")),
            P(("groups", "tm")),
            P(None, "panel"),
            P("comp", None, "panel"),
            P("comp", None),
        ),
        out_specs=P(("groups", "tm"), "panel"),
        check_vma=False,
    )
```

profile of v0, /device:TPU:0, one launch (start us, length us, event | category | flops | bytes accessed | tf_op | source)
XLA Modules:
  0.0 30.6 jit_solution(5740036892168817569)
XLA Ops:
  0.0 28.9 %shard_map.73 = (f32[128,256]{1,0:T(8,128)}, f32[128,256]{1,0:T(8,128)}) custom-call(f32[2,1024]{1,0:T(2,128)} %angles_hbm.1, s32[1,1024]{1,0:T(1,128)} %bitcast.1, s32[2,256]{1,0:T(2,128)} %columns_hbm.1, bf16[1,640,256]{2,1,0:T(8,128)(2,1)} %coeffs_hbm.1, s32[1,2049]{1,0:T(1,128)} %psd_hbm.1, f32[4,256,256]{2,1,0:T(8,128)} %constant.4.clone.square_hbm, ...), custom_call_target="tpu_custom_call" | custom-call | tf_op jit(solution)/shard_map/pallas_call | solution.py:562
  28.9 1.6 %add.3 = f32[128,256]{1,0:T(8,128)} add(f32[128,256]{1,0:T(8,128)} %get-tuple-element.7, f32[128,256]{1,0:T(8,128)} %get-tuple-element.8) | non-fusion elementwise | flops 32768 | bytes 393216 | tf_op jit(solution)/shard_map/add | solution.py:600
where the time goes:
time: 30.8 us; the launch traced here: 30.6 us
  Pallas kernels  28.9 us (94%)
  other arithmetic  1.64 us (5%)
    pallas_call x1, Pallas kernels, fused(): pl.pallas_call(functools.partial(kernel, devices_tm), out_shape=[jax.Shap...  28.9 us
    add x1, other arithmetic, fused(): return own + other  1.64 us

commit v1 on v0

--- a/solution.py
+++ b/solution.py
@@ -158,11 +158,12 @@
 )
 CLASSES = (2, 4, 6, 1, 5, 9, 13)
 EVEN = 3
+ROUNDER = 1.5 * 2.0**23
 MESH = pl.DeviceIdType.MESH
 
 
 def cos_turns(turns, terms=SINE_FINE):
-    offset = turns - jnp.round(turns)
+    offset = turns - ((turns + ROUNDER) - ROUNDER)
     near = 0.25 - jnp.abs(offset)
     square = near * near
     total = terms[-1]
@@ -294,12 +295,11 @@
     twiddle_hbm,
     own_ref,
     other_ref,
-    angles_ref,
-    mask_ref,
     columns_ref,
     coeffs_ref,
     psd_ref,
     orbit,
+    flags,
     far_coeffs,
     far_columns,
     coeffs_t,
@@ -322,7 +322,7 @@
     side_recv,
     load_sem,
 ):
-    block = angles_ref.shape[1]
+    block = angles_hbm.shape[1]
     samples = block * devices_tm
     length = samples // RADIX
     half = length // 2
@@ -335,12 +335,19 @@
     panel = lax.axis_index("panel")
     comp = lax.axis_index("comp")
 
+    barrier = pltpu.get_barrier_semaphore()
+    peers = [lax.rem(me + k, devices_tm) for k in range(1, devices_tm)]
+    for peer in peers:
+        pl.semaphore_signal(barrier, inc=1, device_id={"tm": peer}, device_id_type=MESH)
+    pl.semaphore_signal(barrier, inc=1, device_id={"panel": 1 - panel}, device_id_type=MESH)
+    pl.semaphore_signal(barrier, inc=1, device_id={"comp": 1 - comp}, device_id_type=MESH)
+
     loads = [
         pltpu.make_async_copy(source, held, load_sem.at[i])
         for i, (source, held) in enumerate(
             (
-                (angles_hbm, angles_ref),
-                (mask_hbm, mask_ref),
+                (angles_hbm, orbit.at[me]),
+                (mask_hbm, flags.at[me]),
                 (columns_hbm, columns_ref),
                 (coeffs_hbm, coeffs_ref),
                 (psd_hbm, psd_ref),
@@ -351,31 +358,24 @@
     ]
     for load in loads:
         load.start()
-    barrier = pltpu.get_barrier_semaphore()
-    peers = [lax.rem(me + k, devices_tm) for k in range(1, devices_tm)]
-    for peer in peers:
-        pl.semaphore_signal(barrier, inc=1, device_id={"tm": peer}, device_id_type=MESH)
-    pl.semaphore_signal(barrier, inc=1, device_id={"panel": 1 - panel}, device_id_type=MESH)
-    pl.semaphore_signal(barrier, inc=1, device_id={"comp": 1 - comp}, device_id_type=MESH)
-
-    loads[0].wait()
-    loads[1].wait()
-    orbit[me, 0:2, :] = angles_ref[...] * (0.5 / math.pi)
-    orbit[me, 2:3, :] = mask_ref[...].astype(jnp.float32)
     pl.semaphore_wait(barrier, devices_tm + 1)
 
     def send_orbit(k, slot, peer):
-        return pltpu.make_async_remote_copy(
-            src_ref=orbit.at[slot],
-            dst_ref=orbit.at[slot],
-            send_sem=send_sem.at[k],
-            recv_sem=recv_sem.at[slot],
-            device_id={"tm": peer},
-            device_id_type=MESH,
-        )
+        return [
+            pltpu.make_async_remote_copy(
+                src_ref=source,
+                dst_ref=held.at[slot],
+                send_sem=send_sem.at[i, k],
+                recv_sem=recv_sem.at[i, slot],
+                device_id={"tm": peer},
+                device_id_type=MESH,
+            )
+            for i, (source, held) in enumerate(((angles_hbm, orbit), (mask_hbm, flags)))
+        ]
 
     for k, peer in enumerate(peers):
-        send_orbit(k, me, peer).start()
+        for copy in send_orbit(k, me, peer):
+            copy.start()
     first_row = me * rows
     lanes = pl.ds(pl.multiple_of(lax.rem(first_row, columns), rows), rows)
     send_coeffs = pltpu.make_async_remote_copy(
@@ -439,20 +439,24 @@
         jnp.where(mine, near, far_coeffs[...].astype(jnp.float32)),
         jnp.where(mine, columns_ref[:, lanes], far_columns[...]),
     )
+    loads[0].wait()
+    loads[1].wait()
     for k, peer in enumerate(peers):
-        send_orbit(k, me, peer).wait_send()
-    for k, peer in enumerate(peers):
-        send_orbit(k, peer, peer).wait_recv()
+        for copy in send_orbit(k, me, peer):
+            copy.wait_send()
+        for copy in send_orbit(k, peer, peer):
+            copy.wait_recv()
 
     per_device = block // length
 
-    def epoch_rows(chunk):
-        where = pl.ds(pl.multiple_of(lax.rem(chunk, per_device) * length, length), length)
-        return orbit[chunk // per_device, :, where]
+    def epoch_lanes(chunk):
+        at = lax.rem(chunk, per_device) * length
+        return chunk // per_device, pl.ds(pl.multiple_of(at, length), length)
 
     def fill_basis(chunk, basis):
-        part = epoch_rows(chunk)
-        theta, keep = part[0:1], part[2:3]
+        holder, lanes = epoch_lanes(chunk)
+        theta = orbit[holder, 0:1, lanes] * (0.5 / math.pi)
+        keep = flags[holder, :, lanes].astype(jnp.float32)
         turns = iota((16, length), 0).astype(jnp.float32) * theta
         cosine, sine = cos_turns(turns) * keep, cos_turns(turns - 0.25) * keep
         step_c, step_s = cos_turns(16.0 * theta), cos_turns(16.0 * theta - 0.25)
@@ -462,13 +466,14 @@
             cosine, sine = cosine * step_c - sine * step_s, sine * step_c + cosine * step_s
 
     def fill_design(chunk, basis):
-        longit = epoch_rows(chunk)[1:2]
+        holder, lanes = epoch_lanes(chunk)
+        longit = orbit[holder, 1:2, lanes] * (0.5 / math.pi)
         latitude = jnp.dot(coeffs_t[...], basis[...], preferred_element_type=jnp.float32)
         terms_lon = [column_t[2 + i] for i in range(len(SINE_LON))]
         for lane in range(0, length, 128):
-            lanes = slice(lane, lane + 128)
-            wave = cos_turns(column_t[0] * longit[:, lanes] - column_t[1], terms_lon)
-            design[chunk, :, lanes] = latitude[:, lanes] * wave
+            where = slice(lane, lane + 128)
+            wave = cos_turns(column_t[0] * longit[:, where] - column_t[1], terms_lon)
+            design[chunk, :, where] = latitude[:, where] * wave
 
     fill_basis(0, basis_a)
 
@@ -514,7 +519,7 @@
             jnp.concatenate([parts, high], axis=1), matrix, preferred_element_type=jnp.float32
         ).astype(jnp.bfloat16)
         weighted = (spectra[:columns].astype(jnp.float32) * weight).astype(jnp.bfloat16)
-        return lax.dot_general(
+        total[...] += lax.dot_general(
             spectra[columns:], weighted, (((1,), (1,)), ((), ())), preferred_element_type=jnp.float32
         )
 
@@ -522,19 +527,23 @@
     units = everyone // 16 // EVEN
 
     def even_step(slot, carry):
-        total[...] += gram(pair_even[slot], mat[...], wts[pl.ds(slot + 2, 1), :])
-        for unit in range(units):
-            fold_odd(slot * units + unit)
+        for part in range(2):
+            lanes = slice(part * length, (part + 1) * length)
+            gram(pair_even[slot], mat[:, lanes], wts[pl.ds(slot + 2, 1), lanes])
+            for unit in range(part * units // 2, (part + 1) * units // 2):
+                fold_odd(slot * units + unit)
         return carry
 
     def odd_step(slot, carry):
-        total[...] += gram(pair_odd[slot], mat[...], wts[pl.ds(slot + 2 + EVEN, 1), :])
+        for part in range(2):
+            lanes = slice(part * length, (part + 1) * length)
+            gram(pair_odd[slot], mat[:, lanes], wts[pl.ds(slot + 2 + EVEN, 1), lanes])
         return carry
 
     lax.fori_loop(0, EVEN, even_step, 0)
     lax.fori_loop(0, len(CLASSES) - EVEN, odd_step, 0)
     for slot in range(2):
-        total[...] += gram(real[slot], mat_real[slot], wts[slot : slot + 1, 0:length])
+        gram(real[slot], mat_real[slot], wts[slot : slot + 1, 0:length])
     swap = pltpu.make_async_remote_copy(
         src_ref=total,
         dst_ref=other_ref,
@@ -565,12 +574,11 @@
         in_specs=[pl.BlockSpec(memory_space=pltpu.HBM)] * 7,
         out_specs=[vmem] * 2,
         scratch_shapes=[
-            pltpu.VMEM(orbit_angles.shape, f32),
-            pltpu.VMEM((1, block), jnp.int32),
             pltpu.VMEM(column_index.shape, jnp.int32),
             pltpu.VMEM(lat_coeffs.shape, bf16),
             pltpu.VMEM(psd_table.shape, jnp.int32),
-            pltpu.VMEM((devices_tm, 8, block), f32),
+            pltpu.VMEM((devices_tm, 2, block), f32),
+            pltpu.VMEM((devices_tm, 1, block), jnp.int32),
             pltpu.VMEM((terms, rows), bf16),
             pltpu.VMEM((2, rows), jnp.int32),
             pltpu.VMEM((everyone, terms), bf16),
@@ -587,8 +595,8 @@
             pltpu.VMEM((2 * count, length), f32),
             pltpu.VMEM((16, 2 * length), f32),
             pltpu.VMEM((rows, columns), f32),
-            pltpu.SemaphoreType.DMA((devices_tm,)),
-            pltpu.SemaphoreType.DMA((devices_tm,)),
+            pltpu.SemaphoreType.DMA((2, devices_tm)),
+            pltpu.SemaphoreType.DMA((2, devices_tm)),
             pltpu.SemaphoreType.DMA((3,)),
             pltpu.SemaphoreType.DMA((3,)),
             pltpu.SemaphoreType.DMA((7,)),

time: 30.8 us -> 31 us (level)
  Pallas kernels: 28.9 us -> 29.3 us
    pallas_call x1, Pallas kernels: 28.9 us -> 29.3 us  [fused(): pl.pallas_call(functools.partial(kernel, devices_tm), out_shape=[jax.Shap...]
where the time goes in v1:
time: 31 us; the launch traced here: 30.9 us
  Pallas kernels  29.3 us (95%)
  other arithmetic  1.64 us (5%)
    pallas_call x1, Pallas kernels, fused(): pl.pallas_call(functools.partial(kernel, devices_tm), out_shape=[jax.Shap...  29.3 us
    add x1, other arithmetic, fused(): return own + other  1.64 us

profile of v1, /device:TPU:0, one launch (start us, length us, event | category | flops | bytes accessed | tf_op | source)
XLA Modules:
  0.0 30.9 jit_solution(16414953134123875822)
XLA Ops:
  0.0 29.3 %shard_map.73 = (f32[128,256]{1,0:T(8,128)}, f32[128,256]{1,0:T(8,128)}) custom-call(f32[2,1024]{1,0:T(2,128)} %angles_hbm.1, s32[1,1024]{1,0:T(1,128)} %bitcast.1, s32[2,256]{1,0:T(2,128)} %columns_hbm.1, bf16[1,640,256]{2,1,0:T(8,128)(2,1)} %coeffs_hbm.1, s32[1,2049]{1,0:T(1,128)} %psd_hbm.1, f32[4,256,256]{2,1,0:T(8,128)} %constant.4.clone.square_hbm, ...), custom_call_target="tpu_custom_call" | custom-call | tf_op jit(solution)/shard_map/pallas_call | solution.py:571
  29.3 1.6 %add.3 = f32[128,256]{1,0:T(8,128)} add(f32[128,256]{1,0:T(8,128)} %get-tuple-element.7, f32[128,256]{1,0:T(8,128)} %get-tuple-element.8) | non-fusion elementwise | flops 32768 | bytes 393216 | tf_op jit(solution)/shard_map/add | solution.py:608

commit v2 on v1

--- a/solution.py
+++ b/solution.py
@@ -310,6 +310,7 @@
     real,
     pair_even,
     pair_odd,
+    spectra_even,
     mat_real,
     mat,
     square,
@@ -406,7 +407,6 @@
     put_matrix(mat_real.at[0], 0, square[2], left)
     put_matrix(mat_real.at[1], 0, square[3], left)
     loads[4].wait()
-    frequency_weights(psd_ref, wts, samples)
 
     def place(at, coeffs, index_rows):
         width = coeffs.shape[1]
@@ -513,37 +513,38 @@
     loads[5].wait()
     lax.fori_loop(0, everyone // 16, fold_even, 0)
 
-    def gram(parts, matrix, weight):
+    def spectra_of(parts, matrix):
         high = parts[:, : parts.shape[1] // 2]
-        spectra = jnp.dot(
+        return jnp.dot(
             jnp.concatenate([parts, high], axis=1), matrix, preferred_element_type=jnp.float32
         ).astype(jnp.bfloat16)
+
+    def gram(spectra, weight):
         weighted = (spectra[:columns].astype(jnp.float32) * weight).astype(jnp.bfloat16)
-        total[...] += lax.dot_general(
+        return lax.dot_general(
             spectra[columns:], weighted, (((1,), (1,)), ((), ())), preferred_element_type=jnp.float32
         )
 
-    total[...] = jnp.zeros_like(total)
     units = everyone // 16 // EVEN
 
     def even_step(slot, carry):
-        for part in range(2):
-            lanes = slice(part * length, (part + 1) * length)
-            gram(pair_even[slot], mat[:, lanes], wts[pl.ds(slot + 2, 1), lanes])
-            for unit in range(part * units // 2, (part + 1) * units // 2):
-                fold_odd(slot * units + unit)
+        spectra_even[slot] = spectra_of(pair_even[slot], mat[...])
+        for unit in range(units):
+            fold_odd(slot * units + unit)
         return carry
 
-    def odd_step(slot, carry):
-        for part in range(2):
-            lanes = slice(part * length, (part + 1) * length)
-            gram(pair_odd[slot], mat[:, lanes], wts[pl.ds(slot + 2 + EVEN, 1), lanes])
-        return carry
-
     lax.fori_loop(0, EVEN, even_step, 0)
-    lax.fori_loop(0, len(CLASSES) - EVEN, odd_step, 0)
+    frequency_weights(psd_ref, wts, samples)
+    summed = jnp.zeros((rows, columns), jnp.float32)
+    for slot in range(len(CLASSES) - EVEN):
+        spectra = spectra_of(pair_odd[slot], mat[...])
+        summed = summed + gram(spectra, wts[slot + 2 + EVEN : slot + 3 + EVEN, :])
     for slot in range(2):
-        gram(real[slot], mat_real[slot], wts[slot : slot + 1, 0:length])
+        spectra = spectra_of(real[slot], mat_real[slot])
+        summed = summed + gram(spectra, wts[slot : slot + 1, 0:length])
+    for slot in range(EVEN):
+        summed = summed + gram(spectra_even[slot], wts[slot + 2 : slot + 3, :])
+    total[...] = summed
     swap = pltpu.make_async_remote_copy(
         src_ref=total,
         dst_ref=other_ref,
@@ -589,6 +590,7 @@
             pltpu.VMEM((2, everyone, 2 * length), bf16),
             pltpu.VMEM((EVEN, everyone, 4 * length), bf16),
             pltpu.VMEM((count - EVEN, everyone, 4 * length), bf16),
+            pltpu.VMEM((EVEN, everyone, 2 * length), bf16),
             pltpu.VMEM((2, 3 * length, length), bf16),
             pltpu.VMEM((6 * length, 2 * length), bf16),
             pltpu.VMEM((4, length, length), f32),

time: 31 us -> 30.6 us (0.987)
  Pallas kernels: 29.3 us -> 28.8 us
    pallas_call x1, Pallas kernels: 29.3 us -> 28.8 us  [fused(): pl.pallas_call(functools.partial(kernel, devices_tm), out_shape=[jax.Shap...]
where the time goes in v2:
time: 30.6 us; the launch traced here: 30.5 us
  Pallas kernels  28.8 us (94%)
  other arithmetic  1.64 us (5%)
    pallas_call x1, Pallas kernels, fused(): pl.pallas_call(functools.partial(kernel, devices_tm), out_shape=[jax.Shap...  28.8 us
    add x1, other arithmetic, fused(): return own + other  1.64 us

profile of v2, /device:TPU:0, one launch (start us, length us, event | category | flops | bytes accessed | tf_op | source)
XLA Modules:
  0.0 30.5 jit_solution(5178730983915111275)
XLA Ops:
  0.0 28.8 %shard_map.73 = (f32[128,256]{1,0:T(8,128)}, f32[128,256]{1,0:T(8,128)}) custom-call(f32[2,1024]{1,0:T(2,128)} %angles_hbm.1, s32[1,1024]{1,0:T(1,128)} %bitcast.1, s32[2,256]{1,0:T(2,128)} %columns_hbm.1, bf16[1,640,256]{2,1,0:T(8,128)(2,1)} %coeffs_hbm.1, s32[1,2049]{1,0:T(1,128)} %psd_hbm.1, f32[4,256,256]{2,1,0:T(8,128)} %constant.4.clone.square_hbm, ...), custom_call_target="tpu_custom_call" | custom-call | tf_op jit(solution)/shard_map/pallas_call | solution.py:572
  28.9 1.6 %add.3 = f32[128,256]{1,0:T(8,128)} add(f32[128,256]{1,0:T(8,128)} %get-tuple-element.7, f32[128,256]{1,0:T(8,128)} %get-tuple-element.8) | non-fusion elementwise | flops 32768 | bytes 393216 | tf_op jit(solution)/shard_map/add | solution.py:610

commit v3 on v2

--- a/solution.py
+++ b/solution.py
@@ -430,6 +430,62 @@
     loads[2].wait()
     loads[3].wait()
     place(0, coeffs_ref[0].astype(jnp.float32), columns_ref[...])
+    loads[0].wait()
+    loads[1].wait()
+    per_device = block // length
+
+    def epoch_lanes(chunk):
+        at = lax.rem(chunk, per_device) * length
+        return chunk // per_device, pl.ds(pl.multiple_of(at, length), length)
+
+    def fill_basis(chunk, basis, slot):
+        holder, lanes = epoch_lanes(chunk)
+        theta = orbit[holder, 0:1, lanes] * (0.5 / math.pi)
+        keep = flags[holder, :, lanes].astype(jnp.float32)
+        turns = iota((16, length), 0).astype(jnp.float32) * theta
+        cosine, sine = cos_turns(turns) * keep, cos_turns(turns - 0.25) * keep
+        step_c, step_s = cos_turns(16.0 * theta), cos_turns(16.0 * theta - 0.25)
+        for at in range(0, terms_lat, 16):
+            basis[slot, at : at + 16, :] = cosine.astype(jnp.bfloat16)
+            basis[slot, terms_lat + at : terms_lat + at + 16, :] = sine.astype(jnp.bfloat16)
+            cosine, sine = cosine * step_c - sine * step_s, sine * step_c + cosine * step_s
+
+    def fill_design(chunk, basis, slot, at, width):
+        holder, lanes = epoch_lanes(chunk)
+        longit = orbit[holder, 1:2, lanes] * (0.5 / math.pi)
+        these = slice(at, at + width)
+        latitude = jnp.dot(coeffs_t[these, :], basis[slot], preferred_element_type=jnp.float32)
+        terms_lon = [column_t[2 + i, these, :] for i in range(len(SINE_LON))]
+        for lane in range(0, length, 128):
+            where = slice(lane, lane + 128)
+            wave = cos_turns(
+                column_t[0, these, :] * longit[:, where] - column_t[1, these, :], terms_lon
+            )
+            design[chunk, these, where] = latitude[:, where] * wave
+
+    own_chunks = me * per_device
+
+    def near_columns(first, last):
+        def two_chunks(i, carry):
+            chunk = lax.rem(own_chunks + 2 * i, RADIX)
+            again = jnp.where(i + 1 < last, i + 1, first)
+            fill_basis(chunk + 1, basis_b, i)
+            fill_design(chunk, basis_a, i, 0, columns)
+            fill_basis(lax.rem(own_chunks + 2 * again, RADIX), basis_a, again)
+            fill_design(chunk + 1, basis_b, i, 0, columns)
+            return carry
+
+        fill_basis(lax.rem(own_chunks + 2 * first, RADIX), basis_a, first)
+        lax.fori_loop(first, last, two_chunks, 0)
+
+    near_columns(0, per_device // 2)
+    for k, peer in enumerate(peers):
+        for copy in send_orbit(k, me, peer):
+            copy.wait_send()
+        for copy in send_orbit(k, peer, peer):
+            copy.wait_recv()
+
+    near_columns(per_device // 2, RADIX // 2)
     send_coeffs.wait()
     send_columns.wait()
     mine = first_row // columns == panel
@@ -439,52 +495,14 @@
         jnp.where(mine, near, far_coeffs[...].astype(jnp.float32)),
         jnp.where(mine, columns_ref[:, lanes], far_columns[...]),
     )
-    loads[0].wait()
-    loads[1].wait()
-    for k, peer in enumerate(peers):
-        for copy in send_orbit(k, me, peer):
-            copy.wait_send()
-        for copy in send_orbit(k, peer, peer):
-            copy.wait_recv()
-
-    per_device = block // length
-
-    def epoch_lanes(chunk):
-        at = lax.rem(chunk, per_device) * length
-        return chunk // per_device, pl.ds(pl.multiple_of(at, length), length)
-
-    def fill_basis(chunk, basis):
-        holder, lanes = epoch_lanes(chunk)
-        theta = orbit[holder, 0:1, lanes] * (0.5 / math.pi)
-        keep = flags[holder, :, lanes].astype(jnp.float32)
-        turns = iota((16, length), 0).astype(jnp.float32) * theta
-        cosine, sine = cos_turns(turns) * keep, cos_turns(turns - 0.25) * keep
-        step_c, step_s = cos_turns(16.0 * theta), cos_turns(16.0 * theta - 0.25)
-        for at in range(0, terms_lat, 16):
-            basis[at : at + 16, :] = cosine.astype(jnp.bfloat16)
-            basis[terms_lat + at : terms_lat + at + 16, :] = sine.astype(jnp.bfloat16)
-            cosine, sine = cosine * step_c - sine * step_s, sine * step_c + cosine * step_s
-
-    def fill_design(chunk, basis):
-        holder, lanes = epoch_lanes(chunk)
-        longit = orbit[holder, 1:2, lanes] * (0.5 / math.pi)
-        latitude = jnp.dot(coeffs_t[...], basis[...], preferred_element_type=jnp.float32)
-        terms_lon = [column_t[2 + i] for i in range(len(SINE_LON))]
-        for lane in range(0, length, 128):
-            where = slice(lane, lane + 128)
-            wave = cos_turns(column_t[0] * longit[:, where] - column_t[1], terms_lon)
-            design[chunk, :, where] = latitude[:, where] * wave
-
-    fill_basis(0, basis_a)
-
-    def two_chunks(i, carry):
-        fill_basis(2 * i + 1, basis_b)
-        fill_design(2 * i, basis_a)
-        fill_basis(lax.rem(2 * i + 2, RADIX), basis_a)
-        fill_design(2 * i + 1, basis_b)
+
+    def far_rows(i, carry):
+        chunk = lax.rem(own_chunks + 2 * i, RADIX)
+        fill_design(chunk, basis_a, i, columns, rows)
+        fill_design(chunk + 1, basis_b, i, columns, rows)
         return carry
 
-    lax.fori_loop(0, RADIX // 2, two_chunks, 0)
+    lax.fori_loop(0, RADIX // 2, far_rows, 0)
 
     def turn(slot, pair, at, lane, value):
         re, im = value
@@ -584,8 +602,8 @@
             pltpu.VMEM((2, rows), jnp.int32),
             pltpu.VMEM((everyone, terms), bf16),
             pltpu.VMEM((2 + len(SINE_LON), everyone, 128), f32),
-            pltpu.VMEM((terms, length), bf16),
-            pltpu.VMEM((terms, length), bf16),
+            pltpu.VMEM((RADIX // 2, terms, length), bf16),
+            pltpu.VMEM((RADIX // 2, terms, length), bf16),
             pltpu.VMEM((RADIX, everyone, length), f32),
             pltpu.VMEM((2, everyone, 2 * length), bf16),
             pltpu.VMEM((EVEN, everyone, 4 * length), bf16),
@@ -617,7 +635,7 @@
     rows = columns * panels // devices_tm
     fits = (
         samples == 4096
-        and orbit_angles.shape[1] % 256 == 0
+        and orbit_angles.shape[1] % 512 == 0
         and panels == 2
         and lax.axis_size("comp") == 2
         and rows % 128 == 0

time: 30.6 us -> 28.1 us (0.918)
  Pallas kernels: 28.8 us -> 26.3 us
    pallas_call x1, Pallas kernels: 28.8 us -> 26.3 us  [fused(): pl.pallas_call(functools.partial(kernel, devices_tm), out_shape=[jax.Shap...]
where the time goes in v3:
time: 28.1 us; the launch traced here: 28 us
  Pallas kernels  26.3 us (94%)
  other arithmetic  1.64 us (6%)
    pallas_call x1, Pallas kernels, fused(): pl.pallas_call(functools.partial(kernel, devices_tm), out_shape=[jax.Shap...  26.3 us
    add x1, other arithmetic, fused(): return own + other  1.64 us

profile of v3, /device:TPU:0, one launch (start us, length us, event | category | flops | bytes accessed | tf_op | source)
XLA Modules:
  0.0 28.0 jit_solution(11643600546543326319)
XLA Ops:
  0.0 26.3 %shard_map.73 = (f32[128,256]{1,0:T(8,128)}, f32[128,256]{1,0:T(8,128)}) custom-call(f32[2,1024]{1,0:T(2,128)} %angles_hbm.1, s32[1,1024]{1,0:T(1,128)} %bitcast.1, s32[2,256]{1,0:T(2,128)} %columns_hbm.1, bf16[1,640,256]{2,1,0:T(8,128)(2,1)} %coeffs_hbm.1, s32[1,2049]{1,0:T(1,128)} %psd_hbm.1, f32[4,256,256]{2,1,0:T(8,128)} %constant.4.clone.square_hbm, ...), custom_call_target="tpu_custom_call" | custom-call | tf_op jit(solution)/shard_map/pallas_call | solution.py:590
  26.4 1.6 %add.3 = f32[128,256]{1,0:T(8,128)} add(f32[128,256]{1,0:T(8,128)} %get-tuple-element.7, f32[128,256]{1,0:T(8,128)} %get-tuple-element.8) | non-fusion elementwise | flops 32768 | bytes 393216 | tf_op jit(solution)/shard_map/add | solution.py:628

commit v4 on v3

--- a/solution.py
+++ b/solution.py
@@ -359,45 +359,6 @@
     ]
     for load in loads:
         load.start()
-    pl.semaphore_wait(barrier, devices_tm + 1)
-
-    def send_orbit(k, slot, peer):
-        return [
-            pltpu.make_async_remote_copy(
-                src_ref=source,
-                dst_ref=held.at[slot],
-                send_sem=send_sem.at[i, k],
-                recv_sem=recv_sem.at[i, slot],
-                device_id={"tm": peer},
-                device_id_type=MESH,
-            )
-            for i, (source, held) in enumerate(((angles_hbm, orbit), (mask_hbm, flags)))
-        ]
-
-    for k, peer in enumerate(peers):
-        for copy in send_orbit(k, me, peer):
-            copy.start()
-    first_row = me * rows
-    lanes = pl.ds(pl.multiple_of(lax.rem(first_row, columns), rows), rows)
-    send_coeffs = pltpu.make_async_remote_copy(
-        src_ref=coeffs_hbm.at[0, :, lanes],
-        dst_ref=far_coeffs,
-        send_sem=side_send.at[0],
-        recv_sem=side_recv.at[0],
-        device_id={"panel": 1 - panel},
-        device_id_type=MESH,
-    )
-    send_columns = pltpu.make_async_remote_copy(
-        src_ref=columns_hbm.at[:, lanes],
-        dst_ref=far_columns,
-        send_sem=side_send.at[1],
-        recv_sem=side_recv.at[1],
-        device_id={"panel": 1 - panel},
-        device_id_type=MESH,
-    )
-    send_coeffs.start()
-    send_columns.start()
-
     loads[6].wait()
     left, right = slice(0, length), slice(length, 2 * length)
     put_matrix(mat, 0, square[0], left)
@@ -430,6 +391,45 @@
     loads[2].wait()
     loads[3].wait()
     place(0, coeffs_ref[0].astype(jnp.float32), columns_ref[...])
+    pl.semaphore_wait(barrier, devices_tm + 1)
+
+    def send_orbit(k, slot, peer):
+        return [
+            pltpu.make_async_remote_copy(
+                src_ref=source,
+                dst_ref=held.at[slot],
+                send_sem=send_sem.at[i, k],
+                recv_sem=recv_sem.at[i, slot],
+                device_id={"tm": peer},
+                device_id_type=MESH,
+            )
+            for i, (source, held) in enumerate(((angles_hbm, orbit), (mask_hbm, flags)))
+        ]
+
+    for k, peer in enumerate(peers):
+        for copy in send_orbit(k, me, peer):
+            copy.start()
+    first_row = me * rows
+    lanes = pl.ds(pl.multiple_of(lax.rem(first_row, columns), rows), rows)
+    send_coeffs = pltpu.make_async_remote_copy(
+        src_ref=coeffs_hbm.at[0, :, lanes],
+        dst_ref=far_coeffs,
+        send_sem=side_send.at[0],
+        recv_sem=side_recv.at[0],
+        device_id={"panel": 1 - panel},
+        device_id_type=MESH,
+    )
+    send_columns = pltpu.make_async_remote_copy(
+        src_ref=columns_hbm.at[:, lanes],
+        dst_ref=far_columns,
+        send_sem=side_send.at[1],
+        recv_sem=side_recv.at[1],
+        device_id={"panel": 1 - panel},
+        device_id_type=MESH,
+    )
+    send_coeffs.start()
+    send_columns.start()
+
     loads[0].wait()
     loads[1].wait()
     per_device = block // length
@@ -453,15 +453,18 @@
     def fill_design(chunk, basis, slot, at, width):
         holder, lanes = epoch_lanes(chunk)
         longit = orbit[holder, 1:2, lanes] * (0.5 / math.pi)
-        these = slice(at, at + width)
-        latitude = jnp.dot(coeffs_t[these, :], basis[slot], preferred_element_type=jnp.float32)
-        terms_lon = [column_t[2 + i, these, :] for i in range(len(SINE_LON))]
-        for lane in range(0, length, 128):
-            where = slice(lane, lane + 128)
-            wave = cos_turns(
-                column_t[0, these, :] * longit[:, where] - column_t[1, these, :], terms_lon
-            )
-            design[chunk, these, where] = latitude[:, where] * wave
+        latitude = jnp.dot(
+            coeffs_t[at : at + width, :], basis[slot], preferred_element_type=jnp.float32
+        )
+        for row in range(0, width, 32):
+            these = slice(at + row, at + row + 32)
+            for lane in range(0, length, 128):
+                where = slice(lane, lane + 128)
+                wave = cos_turns(
+                    column_t[0, these, :] * longit[:, where] - column_t[1, these, :],
+                    [column_t[2 + i, these, :] for i in range(len(SINE_LON))],
+                )
+                design[chunk, these, where] = latitude[row : row + 32, where] * wave
 
     own_chunks = me * per_device
 

time: 28.1 us -> 28.8 us (1.025)
  Pallas kernels: 26.3 us -> 27 us
    pallas_call x1, Pallas kernels: 26.3 us -> 27 us  [fused(): pl.pallas_call(functools.partial(kernel, devices_tm), out_shape=[jax.Shap...]
where the time goes in v4:
time: 28.8 us; the launch traced here: 28.6 us
  Pallas kernels  27 us (94%)
  other arithmetic  1.64 us (6%)
    pallas_call x1, Pallas kernels, fused(): pl.pallas_call(functools.partial(kernel, devices_tm), out_shape=[jax.Shap...  27 us
    add x1, other arithmetic, fused(): return own + other  1.64 us

profile of v4, /device:TPU:0, one launch (start us, length us, event | category | flops | bytes accessed | tf_op | source)
XLA Modules:
  0.0 28.6 jit_solution(14441125818212434850)
XLA Ops:
  0.0 27.0 %shard_map.73 = (f32[128,256]{1,0:T(8,128)}, f32[128,256]{1,0:T(8,128)}) custom-call(f32[2,1024]{1,0:T(2,128)} %angles_hbm.1, s32[1,1024]{1,0:T(1,128)} %bitcast.1, s32[2,256]{1,0:T(2,128)} %columns_hbm.1, bf16[1,640,256]{2,1,0:T(8,128)(2,1)} %coeffs_hbm.1, s32[1,2049]{1,0:T(1,128)} %psd_hbm.1, f32[4,256,256]{2,1,0:T(8,128)} %constant.4.clone.square_hbm, ...), custom_call_target="tpu_custom_call" | custom-call | tf_op jit(solution)/shard_map/pallas_call | solution.py:593
  27.0 1.6 %add.3 = f32[128,256]{1,0:T(8,128)} add(f32[128,256]{1,0:T(8,128)} %get-tuple-element.7, f32[128,256]{1,0:T(8,128)} %get-tuple-element.8) | non-fusion elementwise | flops 32768 | bytes 393216 | tf_op jit(solution)/shard_map/add | solution.py:631

commit v5 on v3

--- a/solution.py
+++ b/solution.py
@@ -465,27 +465,26 @@
 
     own_chunks = me * per_device
 
-    def near_columns(first, last):
+    def chunks(first, last, width):
         def two_chunks(i, carry):
             chunk = lax.rem(own_chunks + 2 * i, RADIX)
             again = jnp.where(i + 1 < last, i + 1, first)
             fill_basis(chunk + 1, basis_b, i)
-            fill_design(chunk, basis_a, i, 0, columns)
+            fill_design(chunk, basis_a, i, 0, width)
             fill_basis(lax.rem(own_chunks + 2 * again, RADIX), basis_a, again)
-            fill_design(chunk + 1, basis_b, i, 0, columns)
+            fill_design(chunk + 1, basis_b, i, 0, width)
             return carry
 
         fill_basis(lax.rem(own_chunks + 2 * first, RADIX), basis_a, first)
         lax.fori_loop(first, last, two_chunks, 0)
 
-    near_columns(0, per_device // 2)
+    chunks(0, per_device // 2, columns)
     for k, peer in enumerate(peers):
         for copy in send_orbit(k, me, peer):
             copy.wait_send()
         for copy in send_orbit(k, peer, peer):
             copy.wait_recv()
 
-    near_columns(per_device // 2, RADIX // 2)
     send_coeffs.wait()
     send_columns.wait()
     mine = first_row // columns == panel
@@ -495,6 +494,7 @@
         jnp.where(mine, near, far_coeffs[...].astype(jnp.float32)),
         jnp.where(mine, columns_ref[:, lanes], far_columns[...]),
     )
+    chunks(per_device // 2, RADIX // 2, everyone)
 
     def far_rows(i, carry):
         chunk = lax.rem(own_chunks + 2 * i, RADIX)
@@ -502,7 +502,7 @@
         fill_design(chunk + 1, basis_b, i, columns, rows)
         return carry
 
-    lax.fori_loop(0, RADIX // 2, far_rows, 0)
+    lax.fori_loop(0, per_device // 2, far_rows, 0)
 
     def turn(slot, pair, at, lane, value):
         re, im = value

time: 28.1 us -> 29.6 us (1.053)
  Pallas kernels: 26.3 us -> 27.8 us
    pallas_call x1, Pallas kernels: 26.3 us -> 27.8 us  [fused(): pl.pallas_call(functools.partial(kernel, devices_tm), out_shape=[jax.Shap...]
where the time goes in v5:
time: 29.6 us; the launch traced here: 29.4 us
  Pallas kernels  27.8 us (94%)
  other arithmetic  1.64 us (6%)
    pallas_call x1, Pallas kernels, fused(): pl.pallas_call(functools.partial(kernel, devices_tm), out_shape=[jax.Shap...  27.8 us
    add x1, other arithmetic, fused(): return own + other  1.64 us

profile of v5, /device:TPU:0, one launch (start us, length us, event | category | flops | bytes accessed | tf_op | source)
XLA Modules:
  0.0 29.4 jit_solution(676004680168303550)
XLA Ops:
  0.0 27.8 %shard_map.73 = (f32[128,256]{1,0:T(8,128)}, f32[128,256]{1,0:T(8,128)}) custom-call(f32[2,1024]{1,0:T(2,128)} %angles_hbm.1, s32[1,1024]{1,0:T(1,128)} %bitcast.1, s32[2,256]{1,0:T(2,128)} %columns_hbm.1, bf16[1,640,256]{2,1,0:T(8,128)(2,1)} %coeffs_hbm.1, s32[1,2049]{1,0:T(1,128)} %psd_hbm.1, f32[4,256,256]{2,1,0:T(8,128)} %constant.4.clone.square_hbm, ...), custom_call_target="tpu_custom_call" | custom-call | tf_op jit(solution)/shard_map/pallas_call | solution.py:590
  27.8 1.6 %add.3 = f32[128,256]{1,0:T(8,128)} add(f32[128,256]{1,0:T(8,128)} %get-tuple-element.7, f32[128,256]{1,0:T(8,128)} %get-tuple-element.8) | non-fusion elementwise | flops 32768 | bytes 393216 | tf_op jit(solution)/shard_map/add | solution.py:628

commit v6 on v3

--- a/solution.py
+++ b/solution.py
@@ -398,14 +398,6 @@
     send_coeffs.start()
     send_columns.start()
 
-    loads[6].wait()
-    left, right = slice(0, length), slice(length, 2 * length)
-    put_matrix(mat, 0, square[0], left)
-    put_matrix(mat, 0, -square[1], right)
-    put_matrix(mat, length, square[1], left)
-    put_matrix(mat, length, square[0], right)
-    put_matrix(mat_real.at[0], 0, square[2], left)
-    put_matrix(mat_real.at[1], 0, square[3], left)
     loads[4].wait()
 
     def place(at, coeffs, index_rows):
@@ -486,6 +478,14 @@
             copy.wait_recv()
 
     near_columns(per_device // 2, RADIX // 2)
+    loads[6].wait()
+    left, right = slice(0, length), slice(length, 2 * length)
+    put_matrix(mat, 0, square[0], left)
+    put_matrix(mat, 0, -square[1], right)
+    put_matrix(mat, length, square[1], left)
+    put_matrix(mat, length, square[0], right)
+    put_matrix(mat_real.at[0], 0, square[2], left)
+    put_matrix(mat_real.at[1], 0, square[3], left)
     send_coeffs.wait()
     send_columns.wait()
     mine = first_row // columns == panel

time: 28.1 us -> 28.4 us (1.011)
  Pallas kernels: 26.3 us -> 26.6 us
where the time goes in v6:
time: 28.4 us; the launch traced here: 28.2 us
  Pallas kernels  26.6 us (94%)
  other arithmetic  1.64 us (6%)
    pallas_call x1, Pallas kernels, fused(): pl.pallas_call(functools.partial(kernel, devices_tm), out_shape=[jax.Shap...  26.6 us
    add x1, other arithmetic, fused(): return own + other  1.64 us

profile of v6, /device:TPU:0, one launch (start us, length us, event | category | flops | bytes accessed | tf_op | source)
XLA Modules:
  0.0 28.2 jit_solution(5872434435597924888)
XLA Ops:
  0.0 26.6 %shard_map.73 = (f32[128,256]{1,0:T(8,128)}, f32[128,256]{1,0:T(8,128)}) custom-call(f32[2,1024]{1,0:T(2,128)} %angles_hbm.1, s32[1,1024]{1,0:T(1,128)} %bitcast.1, s32[2,256]{1,0:T(2,128)} %columns_hbm.1, bf16[1,640,256]{2,1,0:T(8,128)(2,1)} %coeffs_hbm.1, s32[1,2049]{1,0:T(1,128)} %psd_hbm.1, f32[4,256,256]{2,1,0:T(8,128)} %constant.4.clone.square_hbm, ...), custom_call_target="tpu_custom_call" | custom-call | tf_op jit(solution)/shard_map/pallas_call | solution.py:590
  26.6 1.6 %add.3 = f32[128,256]{1,0:T(8,128)} add(f32[128,256]{1,0:T(8,128)} %get-tuple-element.7, f32[128,256]{1,0:T(8,128)} %get-tuple-element.8) | non-fusion elementwise | flops 32768 | bytes 393216 | tf_op jit(solution)/shard_map/add | solution.py:628
